TPU v7x, 32 devices: a whole 2x2x4 slice. The times are simulated.
32 devices in a mesh: grp: 2 (over y), tok: 16 (over z, x, core).
Axes of the slice: x: 2, y: 2, z: 4, core: 2. Of those that a mesh axis runs over, the one named last changes fastest.
Arguments:
- hidden: bfloat16 [4, 1024, 1536], P('grp', 'tok'), parts along dimension 0
- base_ids: int32 [4, 1024], P('grp', 'tok'), parts along dimension 0, may hold values from 0 to 4, as said below
- attn_gain: bfloat16 [1536], replicated, may hold values from 0.099609375 to 1.8984375
- q_weight: bfloat16 [1536, 768], replicated
- kv_weight: bfloat16 [1536, 384], replicated
- out_weight: bfloat16 [768, 1536], replicated, may hold values from -0.21875 to 0.21875
- head_gain: bfloat16 [1536], replicated, may hold values from 0.099609375 to 1.8984375
- head_weight: bfloat16 [1536, 1536], replicated, may hold values from -0.15625 to 0.15625
- head_bias: float32 [1536], replicated, may hold values from -1 to 1
- track_perm: int32 [1536], replicated, may hold values from 0 to 1535, each once
Outputs:
- combined: float32 [2048, 1536], P(('grp', 'tok')), parts along dimension 0
There are 2 independent parts, one for each index of `grp`. A program takes and returns all parts, laid end to end along the dimension named above; an argument that names none is the same for every part. Nothing has to cross between parts.
Inputs may be any that keep to these rules, and one draw needn't show every extreme that they name: `base_ids`: every eighth token of each strand, from token 0, has a base 0 to 3.
All inputs are finite; a program needn't handle non-finite values.
Results may differ from a plain program's by a relative error of at most 0.0058.
Values may be sent and summed in bfloat16 or wider, within the bound.
A program may use at most 128 MiB of HBM per device.

v0:
```python
import math

import jax
import jax.numpy as jnp
from jax import lax
from jax.sharding import PartitionSpec as P


def swapped(value, axis, distance):
    mask = 2**distance
    pairs = [(source, source ^ mask) for source in range(lax.axis_size(axis))]
    return lax.ppermute(value, axis, pairs)


def normalize(rows, gain):
    widened = rows.astype(jnp.float32)
    return (
        widened
        * lax.rsqrt(jnp.mean(widened * widened, -1, keepdims=True) + 1e-06)
        * gain.astype(jnp.float32)
    )


def attend(running, queries, key_value, usable_flag):
    maxima, totals, accumulated = running
    width_head = queries.shape[2]
    key_rows = key_value[:, :, :width_head]
    value_rows = key_value[:, :, width_head:]
    scores = jnp.einsum("srd,skd->srk", queries, key_rows, preferred_element_type=jnp.float32) * (
        1.0 / math.sqrt(width_head)
    )
    usable = usable_flag[:, None, :] > 0
    scores = jnp.where(usable, scores, jnp.float32(-1e30))
    new_maxima = jnp.maximum(maxima, jnp.max(scores, -1))
    weight_exp = jnp.where(usable, jnp.exp(scores - new_maxima[:, :, None]), jnp.float32(0.0))
    totals = jnp.sum(weight_exp, -1)
    summed = jnp.einsum(
        "srk,skd->srd",
        weight_exp.astype(jnp.bfloat16),
        value_rows,
        preferred_element_type=jnp.float32,
    )
    accumulated = summed
    return (new_maxima, totals, accumulated)


def per_device(
    hidden,
    base_ids,
    attn_gain,
    q_weight,
    kv_weight,
    out_weight,
    head_gain,
    head_weight,
    head_bias,
    track_perm,
):
    tok_rows = hidden.shape[1]
    width_head = kv_weight.shape[1] // 2
    head_count = q_weight.shape[1] // width_head
    bit_count = lax.axis_size("tok").bit_length() - 1
    normed = normalize(hidden, attn_gain).astype(jnp.bfloat16)
    key_value = jnp.einsum(
        "std,de->ste", normed, kv_weight, preferred_element_type=jnp.float32
    ).astype(jnp.bfloat16)
    usable_flag = (base_ids != 4).astype(jnp.bfloat16)
    partner = hidden[1]
    for bit_number in range(bit_count):
        partner = swapped(partner, "tok", bit_number)
    partner = partner[::-1]
    query_source = jnp.stack([normed[0], normalize(partner, attn_gain).astype(jnp.bfloat16)])
    residual_base = jnp.stack([hidden[0], partner])
    queries = jnp.einsum(
        "std,de->ste", query_source, q_weight, preferred_element_type=jnp.float32
    ).astype(jnp.bfloat16)
    queries = queries.reshape(2, tok_rows * head_count, width_head)
    row_count = queries.shape[1]
    start_state = (
        jnp.full((2, row_count), -1e30, jnp.float32),
        jnp.zeros((2, row_count), jnp.float32),
        jnp.zeros((2, row_count, width_head), jnp.float32),
    )
    softmax_state = attend(
        start_state,
        queries,
        lax.all_gather(key_value, "tok", axis=1, tiled=True),
        lax.all_gather(usable_flag, "tok", axis=1, tiled=True),
    )
    maxima, totals, accumulated = softmax_state
    attended = (
        (accumulated / totals[:, :, None])
        .astype(jnp.bfloat16)
        .reshape(2, tok_rows, head_count * width_head)
    )
    residual_sum = residual_base.astype(jnp.float32) + jnp.einsum(
        "ste,ed->std", attended, out_weight, preferred_element_type=jnp.float32
    )
    normed_out = normalize(residual_sum, head_gain).astype(jnp.bfloat16)
    forward_logits = (
        jnp.dot(normed_out[0], head_weight, preferred_element_type=jnp.float32) + head_bias
    )
    reverse_logits = (
        jnp.dot(normed_out[1], head_weight[:, track_perm], preferred_element_type=jnp.float32)
        + head_bias[track_perm]
    )
    forward_pred = jax.nn.softplus(forward_logits).astype(jnp.bfloat16)
    reverse_pred = jax.nn.softplus(reverse_logits).astype(jnp.bfloat16)
    return 0.5 * (forward_pred.astype(jnp.float32) + reverse_pred.astype(jnp.float32))


def solution(mesh):
    placed = (P("grp", "tok", None), P("grp", "tok"), P(), P(), P(), P(), P(), P(), P(), P())
    return jax.shard_map(
        per_device, mesh=mesh, in_specs=placed, out_specs=P(("grp", "tok"), None), check_vma=False
    )
```

profile of v0, /device:TPU:0, one launch (start us, length us, event | category | flops | bytes accessed | tf_op | source)
XLA Modules:
  0.0 100.6 jit_solution(12420879725566651075)
XLA Ops:
  6.5 0.0 all-gather.3.cloned.1.call-start
  6.6 0.8 convert_element_type.55
  7.4 1.2 %fusion.25 = f32[2,64]{1,0:T(2,128)S(1)} fusion(bf16[2,64,1536]{2,1,0:T(8,128)(2,1)} %param.10), kind=kLoop, calls=%fused_computation.31 | loop fusion | flops 589696 | bytes 393728 | tf_op jit(solution)/shard_map/reduce_sum | solution.py:19
  8.6 1.2 %fusion.27 = bf16[2,64,1536]{2,1,0:T(8,128)(2,1)S(1)} fusion(bf16[2,64,1536]{2,1,0:T(8,128)(2,1)} %param.10, f32[1536]{0:T(1024)S(1)} %convert_element_type.55, f32[2,64]{1,0:T(2,128)S(1)} %add_rsqrt_fusion.1), kind=kLoop, calls=%fused_computation.33 | loop fusion | flops 786432 | bytes 793088 | tf_op jit(solution)/shard_map/convert_element_type | solution.py:63
  9.8 0.0 copy-start.3
  9.8 2.4 %fusion.13 = bf16[2,64,384]{2,1,0:T(8,128)(2,1)} fusion(bf16[2,64,1536]{2,1,0:T(8,128)(2,1)S(1)} %fusion.27, bf16[1536,384]{1,0:T(8,128)(2,1)} %param.14), kind=kOutput, calls=%fused_computation.20 | convolution fusion | flops 151044096 | bytes 1671168 | tf_op jit(solution)/shard_map/std,de->ste/dot_general | solution.py:64
  12.2 0.0 all-gather.3.cloned.1.call-update
  12.3 0.5 collective-permute-start
  12.8 1.1 %collective-permute-done = bf16[64,1536]{1,0:T(8,128)(2,1)S(1)} collective-permute-done((bf16[64,1536]{1,0:T(8,128)(2,1)S(1)}, bf16[64,1536]{1,0:T(8,128)(2,1)S(1)}, u32[]{:S(2)}, u32[]{:S(2)}) %collective-permute-start) | collective-permute-done | bytes 196640 | tf_op jit(solution)/shard_map/ppermute | solution.py:12
  13.8 2.9 %collective-permute-start.1 = (bf16[64,1536]{1,0:T(8,128)(2,1)S(1)}, bf16[64,1536]{1,0:T(8,128)(2,1)S(1)}, u32[]{:S(2)}, u32[]{:S(2)}) collective-permute-start(bf16[64,1536]{1,0:T(8,128)(2,1)S(1)} %collective-permute-done), channel_id=1, source_target_pairs={{0,2},{1,3},{2,0},{3,1},{4,6},{5,7},{6,4},{7,5},{8,10},{9,11},{10,... | collective-permute-start | bytes 589832 | tf_op jit(solution)/shard_map/ppermute | solution.py:12
  16.7 20.5 %all-gather = bf16[16,64,2]{1,2,0:T(2,128)(2,1)S(1)} all-gather(bf16[1,64,2]{1,2,0:T(2,128)(2,1)S(1)} %fusion.37), channel_id=1, replica_groups=mesh['grp'=2,'tok'=16] {'tok'}, dimensions={0}, use_global_device_ids=true | all-gather | bytes 4352 | tf_op jit(solution)/shard_map/all_gather | solution.py:88
  37.3 10.9 %collective-permute-done.2 = bf16[64,1536]{1,0:T(8,128)(2,1)} collective-permute-done((bf16[64,1536]{1,0:T(8,128)(2,1)S(1)}, bf16[64,1536]{1,0:T(8,128)(2,1)}, u32[]{:S(2)}, u32[]{:S(2)}) %collective-permute-start.2) | collective-permute-done | bytes 196640 | tf_op jit(solution)/shard_map/ppermute | solution.py:12
  48.2 0.0 copy-start.5
  48.2 6.7 %copy.26 = bf16[1536,1536]{0,1:T(8,128)(2,1)} copy(bf16[1536,1536]{1,0:T(8,128)(2,1)} %param.17) | data formatting | bytes 9437184 | tf_op args[7]
  54.9 0.1 reshape.64
  55.0 0.0 copy-start.1
  55.0 13.3 %gather_fusion = bf16[1536,1536]{1,0:T(8,128)(2,1)} fusion(bf16[1536,1536]{0,1:T(8,128)(2,1)} %copy.26, s32[2048]{0:T(1024)S(1)} %pad_clamp_fusion), kind=kCustom, calls=%fused_computation | custom fusion | bytes 9443328 | tf_op jit(solution)/shard_map/gather | solution.py:104
  68.4 8.4 %gather_fusion.1 = f32[1536]{0:T(1024)S(1)} fusion(f32[1536]{0:T(1024)S(1)} %copy-done.1, s32[2048]{0:T(1024)S(1)} %pad_clamp_fusion), kind=kCustom, calls=%fused_computation.1 | custom fusion | bytes 18432 | tf_op jit(solution)/shard_map/gather | solution.py:105
  76.8 0.3 rev.3
  77.1 0.1 fusion.28
  77.3 0.1 fusion.36
  77.4 2.2 %fusion.10 = bf16[2,64,768]{2,1,0:T(8,128)(2,1)S(1)} fusion(bf16[1536,768]{1,0:T(8,128)(2,1)} %param.13, bf16[1,64,1536]{2,1,0:T(8,128)(2,1)S(1)} %fusion.36, bf16[1,64,1536]{2,1,0:T(8,128)(2,1)S(1)} %slice-done), kind=kOutput, calls=%fused_computation.19 | convolution fusion | flops 302284800 | bytes 2949120 | tf_op jit(solution)/shard_map/std,de->ste/dot_general | solution.py:74
  79.6 1.0 reshape.41
  80.6 2.0 %fusion.4 = (f32[2,256]{1,0:T(2,128)S(1)}, f32[2,256,1024]{2,1,0:T(8,128)S(1)}) fusion(pred[2,1024]{1,0:T(4,128)(4,1)S(1)} %bitcast.40, bf16[2,256,192]{2,1,0:T(8,128)(2,1)} %reshape.41, bf16[2,1024,384]{2,1,0:T(8,128)(2,1)} %all-gather.3.cloned.1.call-done), kind=kOutput, calls=%fused_computation.10 | convolution fusion | flops 202898944 | bytes 3411968 | tf_op jit(solution)/shard_map/srd,skd->srk/dot_general | solution.py:29
  82.6 0.6 fusion.5
  83.2 1.2 %fusion.9 = bf16[2,256,192]{1,2,0:T(8,128)(2,1)S(1)} fusion(f32[2,256,1024]{2,1,0:T(8,128)S(1)} %get-tuple-element.8, bf16[2,1024,384]{2,1,0:T(8,128)(2,1)S(1)} %copy-done.6, f32[2,256]{1,0:T(2,128)S(1)} %broadcast_maximum_fusion, pred[2,1024]{1,0:T(4,128)(4,1)S(1)} %bitcast.42, f32[2,256]{1,0:T(2,128)S(1)} %fusion.5), kind=kOutput, calls=%fused_computation.18 | convolution fusion | flops 204144640 | bytes 3350528 | tf_op jit(solution)/shard_map/srk,skd->srd/dot_general | solution.py:37
  84.4 0.1 copy.25
  84.6 0.3 reshape.42
  84.9 0.6 multiply_reduce_fusion
  85.4 0.2 multiply_convert_fusion
  85.6 3.4 %fusion.31 = bf16[64,1536]{1,0:T(8,128)(2,1)S(1)} fusion(bf16[1536,1536]{1,0:T(8,128)(2,1)} %param.17, bf16[2,64,1536]{2,1,0:T(8,128)(2,1)S(1)} %multiply_convert_fusion, f32[1536]{0:T(1024)S(1)} %copy-done.1), kind=kOutput, calls=%fused_computation.42 | convolution fusion | flops 302776320 | bytes 5120000 | tf_op jit(solution)/shard_map/dot_general | solution.py:101
  89.0 4.7 %add_multiply_fusion = f32[64,1536]{1,0:T(8,128)} fusion(bf16[1536,1536]{1,0:T(8,128)(2,1)} %gather_fusion, bf16[64,1536]{1,0:T(8,128)(2,1)S(1)} %fusion.31, bf16[2,64,1536]{2,1,0:T(8,128)(2,1)S(1)} %multiply_convert_fusion, f32[1536]{0:T(1024)S(1)} %gather_fusion.1), kind=kOutput, calls=%fused_computation.48 | convolution fusion | flops 303169536 | bytes 5513216 | tf_op jit(solution)/shard_map/dot_general | solution.py:104
  (31 shorter events, 0.1 us)
Async XLA Ops:
  6.5 78.3 %copy-start = (bf16[768,1536]{1,0:T(8,128)(2,1)S(1)}, bf16[768,1536]{1,0:T(8,128)(2,1)}, u32[]{:S(2)}) copy-start(bf16[768,1536]{1,0:T(8,128)(2,1)} %param.15) | copy-start | bytes 7077892
  6.5 5.7 %copy-start.2 = (bf16[2,64,1536]{2,1,0:T(8,128)(2,1)S(1)}, bf16[2,64,1536]{2,1,0:T(8,128)(2,1)}, u32[]{:S(2)}) copy-start(bf16[2,64,1536]{2,1,0:T(8,128)(2,1)} %param.10) | copy-start | bytes 1179652
  6.5 10.2 %copy-start.7 = (s32[2,64]{1,0:T(2,128)S(1)}, s32[2,64]{1,0:T(2,128)}, u32[]{:S(2)}) copy-start(s32[2,64]{1,0:T(2,128)} %param.11) | copy-start | bytes 1540
  6.5 30.7 %copy-start.4 = (s32[1536]{0:T(1024)S(1)}, s32[1536]{0:T(1024)}, u32[]{:S(2)}) copy-start(s32[1536]{0:T(1024)} %param.19) | copy-start | bytes 18436
  6.5 74.0 %all-gather.3.cloned.1.call-start = ((), (), s32[]{:S(2)}) async-start(), calls=%async_computation | async-start | bytes 1671168 | tf_op jit(solution)/shard_map/all_gather | solution.py:87
  9.8 45.1 %copy-start.3 = (bf16[2,64,1536]{2,1,0:T(8,128)(2,1)}, bf16[2,64,1536]{2,1,0:T(8,128)(2,1)S(1)}, u32[]{:S(2)}) copy-start(bf16[2,64,1536]{2,1,0:T(8,128)(2,1)S(1)} %fusion.27) | copy-start | bytes 1179652
  12.3 1.6 %collective-permute-start = (bf16[64,1536]{1,0:T(8,128)(2,1)S(1)}, bf16[64,1536]{1,0:T(8,128)(2,1)S(1)}, u32[]{:S(2)}, u32[]{:S(2)}) collective-permute-start(bf16[64,1536]{1,0:T(8,128)(2,1)S(1)} %get-tuple-element.6), channel_id=1, source_target_pairs={{0,1},{1,0},{2,3},{3,2},{4,5},{5,4},{6,7},{7,6},{8,9},{9,8},{10,11... | collective-permute-start | bytes 589832 | tf_op jit(solution)/shard_map/ppermute | solution.py:12
  13.8 23.4 %collective-permute-start.1 = (bf16[64,1536]{1,0:T(8,128)(2,1)S(1)}, bf16[64,1536]{1,0:T(8,128)(2,1)S(1)}, u32[]{:S(2)}, u32[]{:S(2)}) collective-permute-start(bf16[64,1536]{1,0:T(8,128)(2,1)S(1)} %collective-permute-done), channel_id=1, source_target_pairs={{0,2},{1,3},{2,0},{3,1},{4,6},{5,7},{6,4},{7,5},{8,10},{9,11},{10,... | collective-permute-start | bytes 589832 | tf_op jit(solution)/shard_map/ppermute | solution.py:12
  37.3 10.9 %collective-permute-start.2 = (bf16[64,1536]{1,0:T(8,128)(2,1)S(1)}, bf16[64,1536]{1,0:T(8,128)(2,1)}, u32[]{:S(2)}, u32[]{:S(2)}) collective-permute-start(bf16[64,1536]{1,0:T(8,128)(2,1)S(1)} %collective-permute-done.1), channel_id=1, source_target_pairs={{0,4},{1,5},{2,6},{3,7},{4,0},{5,1},{6,2},{7,3},{8,12},{9,13},{10,... | collective-permute-start | bytes 589832 | tf_op jit(solution)/shard_map/ppermute | solution.py:12
  48.2 28.6 %collective-permute-start.3 = (bf16[64,1536]{1,0:T(8,128)(2,1)}, bf16[64,1536]{1,0:T(8,128)(2,1)S(1)}, u32[]{:S(2)}, u32[]{:S(2)}) collective-permute-start(bf16[64,1536]{1,0:T(8,128)(2,1)} %collective-permute-done.2), channel_id=1, source_target_pairs={{0,8},{1,9},{2,10},{3,11},{4,12},{5,13},{6,14},{7,15},{8,0},{9,1},... | collective-permute-start | bytes 589832 | tf_op jit(solution)/shard_map/ppermute | solution.py:12
  48.2 6.8 %copy-start.5 = (bf16[1536]{0:T(1024)(128)(2,1)S(1)}, bf16[1536]{0:T(1024)(128)(2,1)}, u32[]{:S(2)}) copy-start(bf16[1536]{0:T(1024)(128)(2,1)} %param.16) | copy-start | bytes 9220
  55.0 13.4 %copy-start.1 = (f32[1536]{0:T(1024)S(1)}, f32[1536]{0:T(1024)}, u32[]{:S(2)}) copy-start(f32[1536]{0:T(1024)} %param.18) | copy-start | bytes 18436
  68.4 9.0 %slice-start = ((bf16[2,64,1536]{2,1,0:T(8,128)(2,1)}), bf16[1,64,1536]{2,1,0:T(8,128)(2,1)S(1)}, s32[]{:S(2)}) async-start(bf16[2,64,1536]{2,1,0:T(8,128)(2,1)} %copy-done.3), calls=%async_computation.1 | async-start | bytes 393216 | tf_op jit(solution)/shard_map/slice | solution.py:72
  80.6 2.7 %copy-start.6 = (bf16[2,1024,384]{2,1,0:T(8,128)(2,1)S(1)}, bf16[2,1024,384]{2,1,0:T(8,128)(2,1)}, u32[]{:S(2)}) copy-start(bf16[2,1024,384]{2,1,0:T(8,128)(2,1)} %all-gather.3.cloned.1.call-done) | copy-start | bytes 4718596
Sparse Core Ops, SparseCore 0:
  12.3 46.1 all-gather.2
where the time goes:
time: 101 us
  local copies, waits for them, and re-layouts  30.3 us (30%)
  blocking collectives  20.5 us (20%)
  matrix products  16.5 us (16%)
  between operations  13.6 us (13%)
  waiting for transfers between devices  12 us (12%)
  other arithmetic  4.27 us (4%)
  starting transfers between devices  3.42 us (3%)
    all_gather x1, blocking collectives, per_device(): lax.all_gather(usable_flag, 'tok', axis=1, tiled=True)  20.5 us
    gather x1, local copies, waits for them, and re-layouts, per_device(): head_weight[:, track_perm]  13.3 us
    ppermute x4, waiting for transfers between devices, swapped(): return lax.ppermute(value, axis, pairs)  12 us
    gather x1, local copies, waits for them, and re-layouts, per_device(): head_bias[track_perm]  8.38 us
    unnamed x17, local copies, waits for them, and re-layouts  6.74 us
    dot_general x1, matrix products, per_device(): jnp.dot(normed_out[1], head_weight[:, track_perm], preferred_element_type...  4.69 us
    dot_general x1, matrix products, per_device(): jnp.dot(normed_out[0], head_weight, preferred_element_type=jnp.float32)  3.42 us
    ppermute x4, starting transfers between devices, swapped(): return lax.ppermute(value, axis, pairs)  3.39 us
  transfers between devices with their start and end apart: 5, of which 2 were waited for; matrix products, arithmetic and copies ran while one was open for 32% of the time, Pallas kernels for 0%

commit v1 on v0

v1 whole, which is shorter than its diff:
```python
import functools
import math

import jax
import jax.numpy as jnp
from jax import lax
from jax.experimental import pallas as pl
from jax.experimental.pallas import tpu as pltpu
from jax.sharding import PartitionSpec as P

MESH = pl.DeviceIdType.MESH
LANES = 128
FLAG_ROWS = 16


def normalize(rows, gain):
    widened = rows.astype(jnp.float32)
    mean = jnp.mean(widened * widened, -1, keepdims=True)
    return (widened * lax.rsqrt(mean + 1e-06) * gain.astype(jnp.float32)).astype(jnp.bfloat16)


def dot(a, b):
    return jnp.dot(a, b, preferred_element_type=jnp.float32)


def dot_t(a, b):
    return lax.dot_general(a, b, (((1,), (1,)), ((), ())), preferred_element_type=jnp.float32)


def softplus(v):
    return jnp.maximum(v, 0.0) + jnp.log1p(jnp.exp(-jnp.abs(v)))


def kernel(
    n,
    hidden_ref,
    ids_ref,
    attn_gain_ref,
    q_hbm,
    kv_hbm,
    out_hbm,
    head_gain_ref,
    head_hbm,
    bias_ref,
    perm_ref,
    result_ref,
    hid,
    partner_hid,
    kv_w,
    q_w,
    out_w,
    head_w,
    perm_w,
    buf0,
    buf1,
    scores,
    att,
    fwd_pred,
    load_sem,
    out_sem,
    swap_sem,
    recv,
    send_l,
    send_r,
    send_x,
    send_c,
):
    bufs = (buf0, buf1)
    line = n // 4
    rows, width = hid.shape[1], hid.shape[2]
    tracks = head_w.shape[1]
    head_dim = kv_w.shape[1] // 2
    heads = q_w.shape[1] // head_dim
    padded = att.shape[1] // heads
    pad = padded - head_dim
    kv_tiles = kv_w.shape[1] // LANES
    me = lax.axis_index("tok")
    core = lax.rem(me, 2)
    x = lax.rem(me // 2, 2)
    z = me // 4
    left, right = me - 4, me + 4
    across, sibling, partner = me + 2 - 4 * x, me + 1 - 2 * core, n - 1 - me

    def slot(zc, xc, cc):
        return (zc * 2 + xc) * 2 + cc

    loads = [
        pltpu.make_async_copy(hidden_ref, hid, load_sem.at[0]),
        pltpu.make_async_copy(kv_hbm, kv_w, load_sem.at[1]),
        pltpu.make_async_copy(q_hbm, q_w, load_sem.at[2]),
    ]
    loads += [
        pltpu.make_async_copy(
            out_hbm.at[pl.ds(h * head_dim, head_dim)],
            out_w.at[pl.ds(h * padded + pad, head_dim)],
            out_sem.at[h],
        )
        for h in range(heads)
    ]
    loads += [pltpu.make_async_copy(head_hbm, head_w, load_sem.at[3])]
    for load in loads:
        load.start()

    barrier = pltpu.get_barrier_semaphore()

    def greet(device):
        pl.semaphore_signal(barrier, inc=1, device_id={"tok": device}, device_id_type=MESH)

    has_left, has_right = z > 0, z < line - 1
    for device in (across, sibling, partner):
        greet(device)
    pl.when(has_left)(lambda: greet(left))
    pl.when(has_right)(lambda: greet(right))
    pl.semaphore_wait(
        barrier, 3 + has_left.astype(jnp.int32) + has_right.astype(jnp.int32)
    )

    swap = pltpu.make_async_remote_copy(
        src_ref=hidden_ref.at[1],
        dst_ref=partner_hid,
        send_sem=swap_sem.at[0],
        recv_sem=swap_sem.at[1],
        device_id={"tok": partner},
        device_id_type=MESH,
    )
    swap.start()

    def piece(s, index, device, send_sem):
        return pltpu.make_async_remote_copy(
            src_ref=bufs[s].at[index],
            dst_ref=bufs[s].at[index],
            send_sem=send_sem,
            recv_sem=recv.at[s, index],
            device_id={"tok": device},
            device_id_type=MESH,
        )

    def to_left(s, zc):
        return piece(s, slot(zc, x, core), left, send_l.at[s, zc])

    def to_right(s, zc):
        return piece(s, slot(zc, x, core), right, send_r.at[s, zc])

    def to_across(s, zc):
        return piece(s, slot(zc, x, core), across, send_x.at[s, zc])

    def to_sibling(s, zc, xc):
        return piece(s, slot(zc, xc, core), sibling, send_c.at[s, zc * 2 + xc])

    loads[0].wait()
    gain = attn_gain_ref[...]
    normed = normalize(hid[...].reshape(2 * rows, width), gain)
    loads[1].wait()
    key_value = dot(normed, kv_w[...]).astype(jnp.bfloat16)
    flag = jnp.where(ids_ref[...] != 4, 1.0, 0.0).astype(jnp.float32)
    per_tile = LANES // rows
    lane = lax.broadcasted_iota(jnp.int32, (2, LANES), 1)
    start = lax.rem(me, per_tile) * rows
    spread = jnp.concatenate([flag] * per_tile, axis=1)
    spread = jnp.where((lane >= start) & (lane < start + rows), spread, 0.0)
    spread = jnp.concatenate([spread, jnp.zeros((FLAG_ROWS - 2, LANES), jnp.float32)], axis=0)
    buf0[me, pl.ds(kv_tiles * rows, FLAG_ROWS), :] = spread.astype(jnp.bfloat16)
    for s in range(2):
        for j in range(kv_tiles):
            bufs[s][me, pl.ds(j * rows, rows), :] = key_value[
                s * rows : (s + 1) * rows, j * LANES : (j + 1) * LANES
            ]
        pl.when(has_left)(lambda: to_left(s, z).start())
        pl.when(has_right)(lambda: to_right(s, z).start())
        to_across(s, z).start()
        to_sibling(s, z, x).start()

    def project_queries(normed_rows):
        q = dot(normed_rows, q_w[...])
        pieces = []
        inside = lax.broadcasted_iota(jnp.int32, (rows, padded), 1) < head_dim
        for h in range(heads):
            base = h * head_dim // LANES * LANES
            shift = h * head_dim - base
            window = q[:, base : base + padded]
            if shift:
                window = pltpu.roll(window, padded - shift, axis=1)
            pieces.append(jnp.where(inside, window, 0.0))
        return jnp.concatenate(pieces, axis=0).astype(jnp.bfloat16)

    loads[2].wait()
    q0 = project_queries(normed[:rows])

    def build_perm(i, _):
        step = perm_w.shape[0] // 4
        chunk = 128
        for k in range(step // chunk):
            base = i * step + k * chunk
            ids = lax.broadcasted_iota(jnp.int32, (chunk, tracks), 0) + base
            hit = jnp.where(ids == perm_ref[...], 1.0, 0.0)
            perm_w[pl.ds(pl.multiple_of(base, chunk), chunk), :] = hit.astype(jnp.bfloat16)
        return 0

    def hop(d):
        for s in range(2):

            @pl.when(z - d >= 0)
            def _():
                zc = z - d
                to_right(s, zc).wait_recv()
                pl.when(has_right)(lambda: to_right(s, zc).start())
                to_across(s, zc).start()
                to_sibling(s, zc, x).start()

            @pl.when(z + d < line)
            def _():
                zc = z + d
                to_left(s, zc).wait_recv()
                pl.when(has_left)(lambda: to_left(s, zc).start())
                to_across(s, zc).start()
                to_sibling(s, zc, x).start()

    if line <= 4:
        for d in range(1, line):
            hop(d)
            build_perm(d - 1, 0)
        for i in range(line - 1, 4):
            build_perm(i, 0)
    else:

        @pl.loop(1, line)
        def _(d):
            hop(d)

        lax.fori_loop(0, 4, build_perm, 0)
    out_zero = jnp.zeros((pad, width), jnp.bfloat16)
    for h in range(heads):
        out_w[pl.ds(h * padded, pad), :] = out_zero

    for s in range(2):

        @pl.loop(0, line)
        def _(zc):
            piece(s, slot(zc, 1 - x, core), across, send_x.at[s, zc]).wait_recv()
            to_sibling(s, zc, 1 - x).start()

    def wait_sibling(s):
        @pl.loop(0, line)
        def _(zc):
            for xc in range(2):
                piece(
                    s, slot(zc, xc, 1 - core), sibling, send_c.at[s, zc * 2 + xc]
                ).wait_recv()

    keys = n * rows
    chunk_blocks = min(n, 1024 // rows)
    chunk_keys = chunk_blocks * rows
    chunks = n // chunk_blocks
    scale = 1.0 / math.sqrt(head_dim)

    def tiles(s, c, j):
        part = bufs[s][pl.ds(c * chunk_blocks, chunk_blocks), pl.ds(j * rows, rows), :]
        return part.reshape(chunk_keys, LANES)

    def attend(s, q):
        def usable(c):
            at = pl.ds(c * chunk_blocks, chunk_blocks)
            flags = buf0[at, pl.ds(kv_tiles * rows, FLAG_ROWS), :].astype(jnp.float32)
            parts = []
            for g in range(chunk_blocks // per_tile):
                row = flags[g * per_tile, s : s + 1, :]
                for k in range(1, per_tile):
                    row = row + flags[g * per_tile + k, s : s + 1, :]
                parts.append(row)
            return jnp.concatenate(parts, axis=1) > 0.5

        def score(c):
            lhs = jnp.concatenate([tiles(s, c, j) for j in range(padded // LANES)], axis=1)
            return jnp.where(usable(c), dot_t(q, lhs) * scale, -1e30)

        def weigh(c, value, top):
            weight = jnp.where(usable(c), jnp.exp(value - top), 0.0)
            first = kv_tiles - padded // LANES
            rhs = jnp.concatenate([tiles(s, c, j) for j in range(first, kv_tiles)], axis=1)
            return jnp.sum(weight, -1, keepdims=True), dot(weight.astype(jnp.bfloat16), rhs)

        if chunks == 1:
            value = score(0)
            total, summed = weigh(0, value, jnp.max(value, -1, keepdims=True))
        else:

            def first_pass(c, top):
                value = score(c)
                scores[c] = value
                return jnp.maximum(top, jnp.max(value, -1, keepdims=True))

            top = lax.fori_loop(
                0, chunks, first_pass, jnp.full((heads * rows, 1), -1e30, jnp.float32)
            )

            def second_pass(c, state):
                total, summed = weigh(c, scores[c], top)
                return state[0] + total, state[1] + summed

            total, summed = lax.fori_loop(
                0,
                chunks,
                second_pass,
                (
                    jnp.zeros((heads * rows, 1), jnp.float32),
                    jnp.zeros((heads * rows, padded), jnp.float32),
                ),
            )
        inside = lax.broadcasted_iota(jnp.int32, (heads * rows, padded), 1) >= pad
        mixed = jnp.where(inside, summed / total, 0.0).astype(jnp.bfloat16)
        for h in range(heads):
            att[:, pl.ds(h * padded, padded)] = mixed[h * rows : (h + 1) * rows]

    def predict(hidden_rows):
        residual = hidden_rows.astype(jnp.float32) + dot(att[...], out_w[...])
        normed_out = normalize(residual, head_gain_ref[...])
        return softplus(dot(normed_out, head_w[...]) + bias_ref[...]).astype(jnp.bfloat16)

    wait_sibling(0)
    attend(0, q0)
    for load in loads[3:]:
        load.wait()
    fwd_pred[...] = predict(hid[0])
    swap.wait_recv()
    q1 = project_queries(normalize(partner_hid[...], gain))
    wait_sibling(1)
    attend(1, q1)
    rev_pred = predict(partner_hid[...])
    flip = jnp.where(
        lax.broadcasted_iota(jnp.int32, (rows, rows), 0)
        + lax.broadcasted_iota(jnp.int32, (rows, rows), 1)
        == rows - 1,
        1.0,
        0.0,
    ).astype(jnp.bfloat16)
    flipped = dot(flip, rev_pred).astype(jnp.bfloat16)
    result_ref[...] = 0.5 * (fwd_pred[...].astype(jnp.float32) + dot(flipped, perm_w[...]))

    swap.wait_send()
    for s in range(2):

        @pl.loop(0, line)
        def _(zc):
            pl.when(has_right & (zc <= z))(lambda: to_right(s, zc).wait_send())
            pl.when(has_left & (zc >= z))(lambda: to_left(s, zc).wait_send())
            to_across(s, zc).wait_send()
            for xc in range(2):
                to_sibling(s, zc, xc).wait_send()


def per_device(
    hidden,
    base_ids,
    attn_gain,
    q_weight,
    kv_weight,
    out_weight,
    head_gain,
    head_weight,
    head_bias,
    track_perm,
):
    n = lax.axis_size("tok")
    rows, width = hidden.shape[1], hidden.shape[2]
    head_dim = kv_weight.shape[1] // 2
    heads = q_weight.shape[1] // head_dim
    tracks = head_weight.shape[1]
    padded = -(-head_dim // LANES) * LANES
    line = n // 4
    kv_rows = kv_weight.shape[1] // LANES * rows
    chunk_blocks = min(n, 1024 // rows)
    chunks = n // chunk_blocks
    bf16 = jnp.bfloat16
    vmem = pl.BlockSpec(memory_space=pltpu.VMEM)
    hbm = pl.BlockSpec(memory_space=pl.ANY)
    score_shape = (chunks, heads * rows, chunk_blocks * rows) if chunks > 1 else (1, 8, LANES)
    return pl.pallas_call(
        functools.partial(kernel, n),
        out_shape=jax.ShapeDtypeStruct((rows, tracks), jnp.float32),
        in_specs=[hbm, vmem, vmem, hbm, hbm, hbm, vmem, hbm, vmem, vmem],
        out_specs=vmem,
        scratch_shapes=[
            pltpu.VMEM(hidden.shape, bf16),
            pltpu.VMEM((rows, width), bf16),
            pltpu.VMEM(kv_weight.shape, bf16),
            pltpu.VMEM(q_weight.shape, bf16),
            pltpu.VMEM((heads * padded, width), bf16),
            pltpu.VMEM(head_weight.shape, bf16),
            pltpu.VMEM((tracks, tracks), bf16),
            pltpu.VMEM((n, kv_rows + FLAG_ROWS, LANES), bf16),
            pltpu.VMEM((n, kv_rows, LANES), bf16),
            pltpu.VMEM(score_shape, jnp.float32),
            pltpu.VMEM((rows, heads * padded), bf16),
            pltpu.VMEM((rows, tracks), bf16),
            pltpu.SemaphoreType.DMA((4,)),
            pltpu.SemaphoreType.DMA((heads,)),
            pltpu.SemaphoreType.DMA((2,)),
            pltpu.SemaphoreType.DMA((2, n)),
            pltpu.SemaphoreType.DMA((2, line)),
            pltpu.SemaphoreType.DMA((2, line)),
            pltpu.SemaphoreType.DMA((2, line)),
            pltpu.SemaphoreType.DMA((2, 2 * line)),
        ],
        compiler_params=pltpu.CompilerParams(
            collective_id=0, has_side_effects=True, vmem_limit_bytes=60 * 1024 * 1024
        ),
    )(
        hidden,
        base_ids,
        attn_gain.reshape(1, -1),
        q_weight,
        kv_weight,
        out_weight,
        head_gain.reshape(1, -1),
        head_weight,
        head_bias.reshape(1, -1),
        track_perm.reshape(1, -1),
    )


def solution(mesh):
    placed = (P("grp", "tok", None), P("grp", "tok"), P(), P(), P(), P(), P(), P(), P(), P())
    return jax.shard_map(
        per_device, mesh=mesh, in_specs=placed, out_specs=P(("grp", "tok"), None), check_vma=False
    )
```

time: 101 us -> 43.4 us (0.43)
  Pallas kernels: 0 us -> 36.1 us
  local copies, waits for them, and re-layouts: 30.3 us -> 6.92 us
  blocking collectives: 20.5 us -> 0 us
  matrix products: 16.5 us -> 0 us
  between operations: 13.6 us -> 0.01 us
  waiting for transfers between devices: 12 us -> 0 us
  other arithmetic: 4.27 us -> 0 us
  starting transfers between devices: 3.42 us -> 0 us
    pallas_call x0 -> x1, Pallas kernels: none -> 36.1 us  [per_device(): pl.pallas_call(functools.partial(kernel, n), out_shape=jax.ShapeDtypeStru...]
    gather x2 -> x0, local copies, waits for them, and re-layouts: 21.7 us -> none  [the longest x1 13.3 us: per_device(): head_weight[:, track_perm]]
    all_gather x1 -> x0, blocking collectives: 20.5 us -> none  [per_device(): lax.all_gather(usable_flag, 'tok', axis=1, tiled=True)]
    dot_general x7 -> x0, matrix products: 16.5 us -> none  [the longest x1 4.69 us: per_device(): jnp.dot(normed_out[1], head_weight[:, track_perm], preferred_element_type...]
    ppermute x4 -> x0, waiting for transfers between devices: 12 us -> none  [swapped(): return lax.ppermute(value, axis, pairs)]
    unnamed x17 -> x1, local copies, waits for them, and re-layouts: 6.74 us -> 1.77 us
    reshape x2 -> x4, local copies, waits for them, and re-layouts: 1.23 us -> 5.15 us  [the longest x1 1.3 us: per_device(): track_perm.reshape(1, -1)]
    ppermute x4 -> x0, starting transfers between devices: 3.39 us -> none  [swapped(): return lax.ppermute(value, axis, pairs)]
  transfers between devices with their start and end apart: 5 -> 0, of which waited for: 2 -> 0; matrix products, arithmetic and copies ran while one was open for 32% -> 0% of each run, Pallas kernels for 0% -> 0%
where the time goes in v1:
time: 43.4 us; the launch traced here: 43 us
  Pallas kernels  36.1 us (83%)
  local copies, waits for them, and re-layouts  6.92 us (16%)
    pallas_call x1, Pallas kernels, per_device(): pl.pallas_call(functools.partial(kernel, n), out_shape=jax.ShapeDtypeStru...  36.1 us
    unnamed x1, local copies, waits for them, and re-layouts  1.77 us
    reshape x1, local copies, waits for them, and re-layouts, per_device(): track_perm.reshape(1, -1)  1.3 us
    reshape x1, local copies, waits for them, and re-layouts, per_device(): head_bias.reshape(1, -1)  1.29 us
    reshape x1, local copies, waits for them, and re-layouts, per_device(): attn_gain.reshape(1, -1)  1.28 us
    reshape x1, local copies, waits for them, and re-layouts, per_device(): head_gain.reshape(1, -1)  1.27 us

profile of v1, /device:TPU:0, one launch (start us, length us, event | category | flops | bytes accessed | tf_op | source)
XLA Modules:
  0.0 43.0 jit_solution(5435311976914646937)
XLA Ops:
  0.0 1.3 %reshape.12.attn_gain_ref = bf16[1,1536]{1,0:T(2,128)(2,1)} reshape(bf16[1536]{0:T(1024)(128)(2,1)} %param.12) | data formatting | bytes 6144 | tf_op jit(solution)/shard_map/reshape | solution.py:410
  1.3 1.3 %reshape.13.head_gain_ref = bf16[1,1536]{1,0:T(2,128)(2,1)} reshape(bf16[1536]{0:T(1024)(128)(2,1)} %param.16) | data formatting | bytes 6144 | tf_op jit(solution)/shard_map/reshape | solution.py:414
  2.6 1.3 %reshape.14.bias_ref = f32[1,1536]{1,0:T(1,128)} reshape(f32[1536]{0:T(1024)} %param.18) | data formatting | bytes 12288 | tf_op jit(solution)/shard_map/reshape | solution.py:416
  3.8 1.3 %reshape.15.perm_ref = s32[1,1536]{1,0:T(1,128)} reshape(s32[1536]{0:T(1024)} %param.19) | data formatting | bytes 12288 | tf_op jit(solution)/shard_map/reshape | solution.py:417
  5.2 36.1 %shard_map.100 = f32[64,1536]{1,0:T(8,128)} custom-call(bf16[2,64,1536]{2,1,0:T(8,128)(2,1)} %hidden_ref.1, s32[2,64]{1,0:T(2,128)} %ids_ref.1, bf16[1,1536]{1,0:T(2,128)(2,1)} %reshape.12.attn_gain_ref, bf16[1536,768]{1,0:T(8,128)(2,1)} %q_hbm.1, bf16[1536,384]{1,0:T(8,128)(2,1)} %kv_hbm.1, bf16[768,1536]{1,0:T(8,128)(2,1)} %out_hbm.1, ...), custom_call_target="tpu_custom_call" | custom-call | tf_op jit(solution)/shard_map/pallas_call | solution.py:377
  41.3 1.8 %copy.12 = f32[64,1536]{1,0:T(8,128)} copy(f32[64,1536]{1,0:T(8,128)} %shard_map.100) | data formatting | bytes 786432

commit v2 on v1

v2 whole, which is shorter than its diff:
```python
import functools
import math

import jax
import jax.numpy as jnp
from jax import lax
from jax.experimental import pallas as pl
from jax.experimental.pallas import tpu as pltpu
from jax.sharding import PartitionSpec as P

MESH = pl.DeviceIdType.MESH
LANES = 128
FLAG_ROWS = 16


def normalize(rows, gain):
    widened = rows.astype(jnp.float32)
    mean = jnp.mean(widened * widened, -1, keepdims=True)
    return (widened * lax.rsqrt(mean + 1e-06) * gain.astype(jnp.float32)).astype(jnp.bfloat16)


def dot(a, b):
    return jnp.dot(a, b, preferred_element_type=jnp.float32)


def dot_t(a, b):
    return lax.dot_general(a, b, (((1,), (1,)), ((), ())), preferred_element_type=jnp.float32)


def softplus(v):
    return jnp.maximum(v, 0.0) + jnp.log1p(jnp.exp(-jnp.abs(v)))


def vector(ref):
    return ref[...].reshape(1, -1)


def kernel(
    n,
    hidden_ref,
    ids_ref,
    attn_gain_ref,
    q_hbm,
    kv_hbm,
    out_hbm,
    head_gain_ref,
    head_hbm,
    bias_ref,
    perm_ref,
    result_ref,
    hid,
    work,
    kv_w,
    q_w,
    out_w,
    head_w,
    perm_w,
    buf,
    stage,
    scores,
    att,
    final,
    other,
    load_sem,
    out_sem,
    swap_send,
    work_sem,
    pair_sem,
    final_sem,
    recv,
    send_l,
    send_r,
    send_x,
):
    line = n // 4
    rows, width = hid.shape[1], hid.shape[2]
    both = 2 * rows
    tracks = head_w.shape[1]
    head_dim = kv_w.shape[1] // 2
    heads = q_w.shape[1] // head_dim
    padded = att.shape[1] // heads
    pad = padded - head_dim
    kv_tiles = kv_w.shape[1] // LANES
    me = lax.axis_index("tok")
    core = lax.rem(me, 2)
    x = lax.rem(me // 2, 2)
    z = me // 4
    left, right = me - 4, me + 4
    across, sibling = me + 2 - 4 * x, me + 1 - 2 * core
    mirror_zero, mirror_one = n - 2 - me + core, n - 1 - me + core
    first = core == 0
    second = core == 1
    has_left, has_right = z > 0, z < line - 1

    def slot(zc, xc, cc):
        return (zc * 2 + xc) * 2 + cc

    def remote(src, dst, send_sem, recv_sem, device):
        return pltpu.make_async_remote_copy(
            src_ref=src,
            dst_ref=dst,
            send_sem=send_sem,
            recv_sem=recv_sem,
            device_id={"tok": device},
            device_id_type=MESH,
        )

    load_hid = pltpu.make_async_copy(hidden_ref, hid, load_sem.at[0])
    load_kv = pltpu.make_async_copy(kv_hbm, kv_w, load_sem.at[1])
    load_q = pltpu.make_async_copy(q_hbm, q_w, load_sem.at[2])
    load_head = pltpu.make_async_copy(head_hbm, head_w, load_sem.at[3])
    load_out = [
        pltpu.make_async_copy(
            out_hbm.at[pl.ds(h * head_dim, head_dim)],
            out_w.at[pl.ds(h * padded + pad, head_dim)],
            out_sem.at[h],
        )
        for h in range(heads)
    ]
    for load in [load_hid, load_kv, load_q] + load_out + [load_head]:
        load.start()

    barrier = pltpu.get_barrier_semaphore()

    def greet(device):
        pl.semaphore_signal(barrier, inc=1, device_id={"tok": device}, device_id_type=MESH)

    greet(sibling)
    greet(across)
    pl.when(has_left)(lambda: greet(left))
    pl.when(has_right)(lambda: greet(right))

    @pl.when(second)
    def _():
        greet(mirror_zero)
        greet(mirror_one)

    pl.semaphore_wait(barrier, 3 + has_left.astype(jnp.int32) + has_right.astype(jnp.int32))

    lower, upper = work.at[pl.ds(0, rows)], work.at[pl.ds(rows, rows)]
    keep_own = pltpu.make_async_copy(hidden_ref.at[0], lower, work_sem.at[0])
    give_pair = remote(hidden_ref.at[0], upper, swap_send.at[0], work_sem.at[1], sibling)
    swap_lower = remote(hidden_ref.at[1], lower, swap_send.at[1], work_sem.at[0], mirror_one)
    swap_upper = remote(hidden_ref.at[1], upper, swap_send.at[1], work_sem.at[1], mirror_one)

    @pl.when(first)
    def _():
        keep_own.start()
        swap_lower.start()

    @pl.when(second)
    def _():
        give_pair.start()
        swap_upper.start()

    def piece(index, device, send_sem):
        return remote(buf.at[index], buf.at[index], send_sem, recv.at[index], device)

    def to_left(zc, half):
        return piece(slot(zc, x, half), left, send_l.at[half, zc])

    def to_right(zc, half):
        return piece(slot(zc, x, half), right, send_r.at[half, zc])

    def to_across(zc, half):
        return piece(slot(zc, x, half), across, send_x.at[half, zc])

    pair = remote(stage, buf.at[me], pair_sem.at[0], recv.at[me], sibling)
    pair_in = remote(stage, buf.at[sibling], pair_sem.at[0], recv.at[sibling], sibling)

    load_hid.wait()
    gain = vector(attn_gain_ref)
    normed = normalize(hid[...].reshape(both, width), gain)
    load_kv.wait()
    key_value = dot(normed, kv_w[...])
    forward, reverse = key_value[:rows], key_value[rows:]
    mine = jnp.where(first, forward, reverse).astype(jnp.bfloat16)
    theirs = jnp.where(first, reverse, forward).astype(jnp.bfloat16)
    flag = jnp.where(ids_ref[...] != 4, 1.0, 0.0).astype(jnp.float32)
    per_tile = LANES // rows
    lane = lax.broadcasted_iota(jnp.int32, (1, LANES), 1)
    start = lax.rem(me, per_tile) * rows
    inside_tile = (lane >= start) & (lane < start + rows)

    def fill(block, values, flags):
        for j in range(kv_tiles):
            block[pl.ds(j * rows, rows), :] = values[:, j * LANES : (j + 1) * LANES]
        spread = jnp.where(inside_tile, jnp.concatenate([flags] * per_tile, axis=1), 0.0)
        spread = jnp.broadcast_to(spread, (FLAG_ROWS, LANES))
        block[pl.ds(kv_tiles * rows, FLAG_ROWS), :] = spread.astype(jnp.bfloat16)

    fill(stage, theirs, jnp.where(first, flag[1:2], flag[0:1]))
    pair.start()
    fill(buf.at[me], mine, jnp.where(first, flag[0:1], flag[1:2]))

    def spread_out(zc, half, go_left, go_right):
        if go_left:
            pl.when(has_left)(lambda: to_left(zc, half).start())
        if go_right:
            pl.when(has_right)(lambda: to_right(zc, half).start())
        to_across(zc, half).start()

    spread_out(z, core, True, True)
    pair_in.wait_recv()
    spread_out(z, 1 - core, True, True)

    def hop(d):
        for k in range(2):
            half = core if k == 0 else 1 - core

            @pl.when(z - d >= 0)
            def _():
                to_right(z - d, half).wait_recv()
                spread_out(z - d, half, False, True)

            @pl.when(z + d < line)
            def _():
                to_left(z + d, half).wait_recv()
                spread_out(z + d, half, True, False)

    def project_queries(normed_rows):
        q = dot(normed_rows, q_w[...])
        pieces = []
        inside = lax.broadcasted_iota(jnp.int32, (both, padded), 1) < head_dim
        for h in range(heads):
            base = h * head_dim // LANES * LANES
            shift = h * head_dim - base
            window = q[:, base : base + padded]
            if shift:
                window = pltpu.roll(window, padded - shift, axis=1)
            pieces.append(jnp.where(inside, window, 0.0).astype(jnp.bfloat16))
        return pieces

    perm_row = vector(perm_ref)

    def build_perm(i, _):
        step = perm_w.shape[0] // 4
        chunk = 128
        for k in range(step // chunk):
            base = i * step + k * chunk
            ids = lax.broadcasted_iota(jnp.int32, (chunk, tracks), 0) + base
            hit = jnp.where(ids == perm_row, 1.0, 0.0)
            perm_w[pl.ds(pl.multiple_of(base, chunk), chunk), :] = hit.astype(jnp.bfloat16)
        return 0

    out_zero = jnp.zeros((pad, width), jnp.bfloat16)
    for h in range(heads):
        out_w[pl.ds(h * padded, pad), :] = out_zero
    if line <= 4:
        for d in range(1, line):
            hop(d)
            if d < line - 1:
                build_perm(2 * d - 2, 0)
                build_perm(2 * d - 1, 0)
        for i in range(2 * max(line - 2, 0), 4):
            build_perm(i, 0)
    else:
        pl.loop(1, line)(hop)
        lax.fori_loop(0, 4, build_perm, 0)

    load_q.wait()
    pltpu.make_async_copy(hidden_ref.at[0], lower, work_sem.at[0]).wait()
    swap_upper.wait_recv()
    queries = project_queries(normalize(work[...], gain))

    @pl.loop(0, line)
    def _(zc):
        for half in range(2):
            piece(slot(zc, 1 - x, half), across, send_x.at[half, zc]).wait_recv()

    chunk_blocks = min(n, 1024 // rows)
    chunk_keys = chunk_blocks * rows
    chunks = n // chunk_blocks
    scale = 1.0 / math.sqrt(head_dim)

    def tiles(c, low, high):
        at = pl.ds(c * chunk_blocks, chunk_blocks)
        return jnp.concatenate(
            [
                buf[at, pl.ds(j * rows, rows), :].reshape(chunk_keys, LANES)
                for j in range(low, high)
            ],
            axis=1,
        )

    def usable(c):
        at = pl.ds(c * chunk_blocks, chunk_blocks)
        flags = buf[at, pl.ds(kv_tiles * rows, FLAG_ROWS), :].astype(jnp.float32)
        parts = []
        for g in range(chunk_blocks // per_tile):
            row = flags[g * per_tile, 0:1, :]
            for k in range(1, per_tile):
                row = row + flags[g * per_tile + k, 0:1, :]
            parts.append(row)
        return jnp.concatenate(parts, axis=1) > 0.5

    def score(c, q):
        return jnp.where(usable(c), dot_t(q, tiles(c, 0, padded // LANES)) * scale, -1e30)

    def weigh(c, value, top):
        weight = jnp.where(usable(c), jnp.exp(value - top), 0.0)
        rhs = tiles(c, kv_tiles - padded // LANES, kv_tiles)
        return jnp.sum(weight, -1, keepdims=True), dot(weight.astype(jnp.bfloat16), rhs)

    inside = lax.broadcasted_iota(jnp.int32, (both, padded), 1) >= pad
    for h in range(heads):
        if chunks == 1:
            value = score(0, queries[h])
            total, summed = weigh(0, value, jnp.max(value, -1, keepdims=True))
        else:

            def first_pass(c, top):
                value = score(c, queries[h])
                scores[c] = value
                return jnp.maximum(top, jnp.max(value, -1, keepdims=True))

            top = lax.fori_loop(
                0, chunks, first_pass, jnp.full((both, 1), -1e30, jnp.float32)
            )

            def second_pass(c, state):
                total, summed = weigh(c, scores[c], top)
                return state[0] + total, state[1] + summed

            empty = jnp.zeros((both, 1), jnp.float32), jnp.zeros((both, padded), jnp.float32)
            total, summed = lax.fori_loop(0, chunks, second_pass, empty)
        mixed = jnp.where(inside, summed / total, 0.0)
        att[:, pl.ds(h * padded, padded)] = mixed.astype(jnp.bfloat16)

    for load in load_out:
        load.wait()
    residual = work[...].astype(jnp.float32) + dot(att[...], out_w[...])
    normed_out = normalize(residual, vector(head_gain_ref))
    load_head.wait()
    pred = softplus(dot(normed_out, head_w[...]) + vector(bias_ref)).astype(jnp.bfloat16)

    @pl.when(first)
    def _():
        final[...] = pred

    @pl.when(second)
    def _():
        flip = jnp.where(
            lax.broadcasted_iota(jnp.int32, (both, both), 0)
            + lax.broadcasted_iota(jnp.int32, (both, both), 1)
            == both - 1,
            1.0,
            0.0,
        ).astype(jnp.bfloat16)
        flipped = dot(flip, pred).astype(jnp.bfloat16)
        final[...] = dot(flipped, perm_w[...]).astype(jnp.bfloat16)

    own = pl.ds(pl.multiple_of(core * rows, rows), rows)
    far = pl.ds(pl.multiple_of(rows - core * rows, rows), rows)
    exchange = remote(final.at[far], other, final_sem.at[0], final_sem.at[1], sibling)
    exchange.start()
    exchange.wait_recv()
    result_ref[...] = 0.5 * (final[own, :].astype(jnp.float32) + other[...].astype(jnp.float32))

    exchange.wait_send()
    pair.wait_send()
    swap_upper.wait_send()
    pl.when(second)(lambda: give_pair.wait_send())

    @pl.loop(0, line)
    def _(zc):
        for half in range(2):
            pl.when(has_right & (zc <= z))(lambda: to_right(zc, half).wait_send())
            pl.when(has_left & (zc >= z))(lambda: to_left(zc, half).wait_send())
            to_across(zc, half).wait_send()


def per_device(
    hidden,
    base_ids,
    attn_gain,
    q_weight,
    kv_weight,
    out_weight,
    head_gain,
    head_weight,
    head_bias,
    track_perm,
):
    n = lax.axis_size("tok")
    rows, width = hidden.shape[1], hidden.shape[2]
    head_dim = kv_weight.shape[1] // 2
    heads = q_weight.shape[1] // head_dim
    tracks = head_weight.shape[1]
    padded = -(-head_dim // LANES) * LANES
    line = n // 4
    kv_rows = kv_weight.shape[1] // LANES * rows
    chunk_blocks = min(n, 1024 // rows)
    chunks = n // chunk_blocks
    bf16 = jnp.bfloat16
    vmem = pl.BlockSpec(memory_space=pltpu.VMEM)
    hbm = pl.BlockSpec(memory_space=pl.ANY)
    score_shape = (chunks, 2 * rows, chunk_blocks * rows) if chunks > 1 else (1, 8, LANES)
    return pl.pallas_call(
        functools.partial(kernel, n),
        out_shape=jax.ShapeDtypeStruct((rows, tracks), jnp.float32),
        in_specs=[hbm, vmem, vmem, hbm, hbm, hbm, vmem, hbm, vmem, vmem],
        out_specs=vmem,
        scratch_shapes=[
            pltpu.VMEM(hidden.shape, bf16),
            pltpu.VMEM((2 * rows, width), bf16),
            pltpu.VMEM(kv_weight.shape, bf16),
            pltpu.VMEM(q_weight.shape, bf16),
            pltpu.VMEM((heads * padded, width), bf16),
            pltpu.VMEM(head_weight.shape, bf16),
            pltpu.VMEM((tracks, tracks), bf16),
            pltpu.VMEM((n, kv_rows + FLAG_ROWS, LANES), bf16),
            pltpu.VMEM((kv_rows + FLAG_ROWS, LANES), bf16),
            pltpu.VMEM(score_shape, jnp.float32),
            pltpu.VMEM((2 * rows, heads * padded), bf16),
            pltpu.VMEM((2 * rows, tracks), bf16),
            pltpu.VMEM((rows, tracks), bf16),
            pltpu.SemaphoreType.DMA((4,)),
            pltpu.SemaphoreType.DMA((heads,)),
            pltpu.SemaphoreType.DMA((2,)),
            pltpu.SemaphoreType.DMA((2,)),
            pltpu.SemaphoreType.DMA((1,)),
            pltpu.SemaphoreType.DMA((2,)),
            pltpu.SemaphoreType.DMA((n,)),
            pltpu.SemaphoreType.DMA((2, line)),
            pltpu.SemaphoreType.DMA((2, line)),
            pltpu.SemaphoreType.DMA((2, line)),
        ],
        compiler_params=pltpu.CompilerParams(
            collective_id=0, has_side_effects=True, vmem_limit_bytes=60 * 1024 * 1024
        ),
    )(
        hidden,
        base_ids,
        attn_gain,
        q_weight,
        kv_weight,
        out_weight,
        head_gain,
        head_weight,
        head_bias,
        track_perm,
    )


def solution(mesh):
    placed = (P("grp", "tok", None), P("grp", "tok"), P(), P(), P(), P(), P(), P(), P(), P())
    return jax.shard_map(
        per_device, mesh=mesh, in_specs=placed, out_specs=P(("grp", "tok"), None), check_vma=False
    )
```

time: 43.4 us -> 35.1 us (0.81)
  local copies, waits for them, and re-layouts: 6.92 us -> 1.77 us
  Pallas kernels: 36.1 us -> 33.2 us
    reshape x4 -> x0, local copies, waits for them, and re-layouts: 5.15 us -> none  [the longest x1 1.3 us: per_device(): track_perm.reshape(1, -1)]
    pallas_call x1, Pallas kernels: 36.1 us -> 33.2 us  [per_device(): pl.pallas_call(functools.partial(kernel, n), out_shape=jax.ShapeDtypeStru...]
where the time goes in v2:
time: 35.1 us; the launch traced here: 34.9 us
  Pallas kernels  33.2 us (95%)
  local copies, waits for them, and re-layouts  1.77 us (5%)
    pallas_call x1, Pallas kernels, per_device(): pl.pallas_call(functools.partial(kernel, n), out_shape=jax.ShapeDtypeStru...  33.2 us
    unnamed x1, local copies, waits for them, and re-layouts  1.77 us

profile of v2, /device:TPU:0, one launch (start us, length us, event | category | flops | bytes accessed | tf_op | source)
XLA Modules:
  0.0 34.9 jit_solution(4229180490207949704)
XLA Ops:
  0.0 33.2 %shard_map.100 = f32[64,1536]{1,0:T(8,128)} custom-call(bf16[2,64,1536]{2,1,0:T(8,128)(2,1)} %hidden_ref.1, s32[2,64]{1,0:T(2,128)} %ids_ref.1, bf16[1536]{0:T(1024)(128)(2,1)} %attn_gain_ref.1, bf16[1536,768]{1,0:T(8,128)(2,1)} %q_hbm.1, bf16[1536,384]{1,0:T(8,128)(2,1)} %kv_hbm.1, bf16[768,1536]{1,0:T(8,128)(2,1)} %out_hbm.1, ...), custom_call_target="tpu_custom_call" | custom-call | tf_op jit(solution)/shard_map/pallas_call | solution.py:399
  33.2 1.8 %copy.12 = f32[64,1536]{1,0:T(8,128)} copy(f32[64,1536]{1,0:T(8,128)} %shard_map.100) | data formatting | bytes 786432

commit v3 on v2

--- a/solution.py
+++ b/solution.py
@@ -70,6 +70,8 @@
     recv,
     send_l,
     send_r,
+    send_ll,
+    send_rr,
     send_x,
 ):
     line = n // 4
@@ -91,6 +93,9 @@
     first = core == 0
     second = core == 1
     has_left, has_right = z > 0, z < line - 1
+    even = lax.rem(z, 2) == 0
+    odd = lax.rem(z, 2) == 1
+    skip_right, skip_left = even & (z < line - 2), odd & (z > 1)
 
     def slot(zc, xc, cc):
         return (zc * 2 + xc) * 2 + cc
@@ -129,13 +134,16 @@
     greet(across)
     pl.when(has_left)(lambda: greet(left))
     pl.when(has_right)(lambda: greet(right))
+    pl.when(even & (z > 1))(lambda: greet(me - 8))
+    pl.when(odd & (z < line - 2))(lambda: greet(me + 8))
 
     @pl.when(second)
     def _():
         greet(mirror_zero)
         greet(mirror_one)
 
-    pl.semaphore_wait(barrier, 3 + has_left.astype(jnp.int32) + has_right.astype(jnp.int32))
+    peers = [flag.astype(jnp.int32) for flag in (has_left, has_right, skip_left, skip_right)]
+    pl.semaphore_wait(barrier, 3 + sum(peers))
 
     lower, upper = work.at[pl.ds(0, rows)], work.at[pl.ds(rows, rows)]
     keep_own = pltpu.make_async_copy(hidden_ref.at[0], lower, work_sem.at[0])
@@ -162,12 +170,21 @@
     def to_right(zc, half):
         return piece(slot(zc, x, half), right, send_r.at[half, zc])
 
+    def to_left_two(zc, half):
+        return piece(slot(zc, x, half), me - 8, send_ll.at[half, zc])
+
+    def to_right_two(zc, half):
+        return piece(slot(zc, x, half), me + 8, send_rr.at[half, zc])
+
     def to_across(zc, half):
         return piece(slot(zc, x, half), across, send_x.at[half, zc])
 
     pair = remote(stage, buf.at[me], pair_sem.at[0], recv.at[me], sibling)
     pair_in = remote(stage, buf.at[sibling], pair_sem.at[0], recv.at[sibling], sibling)
 
+    out_zero = jnp.zeros((pad, width), jnp.bfloat16)
+    for h in range(heads):
+        out_w[pl.ds(h * padded, pad), :] = out_zero
     load_hid.wait()
     gain = vector(attn_gain_ref)
     normed = normalize(hid[...].reshape(both, width), gain)
@@ -194,10 +211,17 @@
     fill(buf.at[me], mine, jnp.where(first, flag[0:1], flag[1:2]))
 
     def spread_out(zc, half, go_left, go_right):
+        source = go_left and go_right
         if go_left:
-            pl.when(has_left)(lambda: to_left(zc, half).start())
+            pl.when(skip_left)(lambda: to_left_two(zc, half).start())
+            pl.when(has_left if source else has_left & odd)(
+                lambda: to_left(zc, half).start()
+            )
         if go_right:
-            pl.when(has_right)(lambda: to_right(zc, half).start())
+            pl.when(skip_right)(lambda: to_right_two(zc, half).start())
+            pl.when(has_right if source else has_right & even)(
+                lambda: to_right(zc, half).start()
+            )
         to_across(zc, half).start()
 
     spread_out(z, core, True, True)
@@ -243,19 +267,14 @@
             perm_w[pl.ds(pl.multiple_of(base, chunk), chunk), :] = hit.astype(jnp.bfloat16)
         return 0
 
-    out_zero = jnp.zeros((pad, width), jnp.bfloat16)
-    for h in range(heads):
-        out_w[pl.ds(h * padded, pad), :] = out_zero
     if line <= 4:
         for d in range(1, line):
             hop(d)
-            if d < line - 1:
-                build_perm(2 * d - 2, 0)
-                build_perm(2 * d - 1, 0)
-        for i in range(2 * max(line - 2, 0), 4):
-            build_perm(i, 0)
     else:
         pl.loop(1, line)(hop)
+
+    @pl.when(second)
+    def _():
         lax.fori_loop(0, 4, build_perm, 0)
 
     load_q.wait()
@@ -365,8 +384,14 @@
     @pl.loop(0, line)
     def _(zc):
         for half in range(2):
-            pl.when(has_right & (zc <= z))(lambda: to_right(zc, half).wait_send())
-            pl.when(has_left & (zc >= z))(lambda: to_left(zc, half).wait_send())
+            pl.when(has_right & ((zc == z) | (even & (zc < z))))(
+                lambda: to_right(zc, half).wait_send()
+            )
+            pl.when(has_left & ((zc == z) | (odd & (zc > z))))(
+                lambda: to_left(zc, half).wait_send()
+            )
+            pl.when(skip_right & (zc <= z))(lambda: to_right_two(zc, half).wait_send())
+            pl.when(skip_left & (zc >= z))(lambda: to_left_two(zc, half).wait_send())
             to_across(zc, half).wait_send()
 
 
@@ -425,6 +450,8 @@
             pltpu.SemaphoreType.DMA((2, line)),
             pltpu.SemaphoreType.DMA((2, line)),
             pltpu.SemaphoreType.DMA((2, line)),
+            pltpu.SemaphoreType.DMA((2, line)),
+            pltpu.SemaphoreType.DMA((2, line)),
         ],
         compiler_params=pltpu.CompilerParams(
             collective_id=0, has_side_effects=True, vmem_limit_bytes=60 * 1024 * 1024

time: 35.1 us -> 37 us (1.054)
  Pallas kernels: 33.2 us -> 35 us
    pallas_call x1, Pallas kernels: 33.2 us -> 35 us  [per_device(): pl.pallas_call(functools.partial(kernel, n), out_shape=jax.ShapeDtypeStru...]
where the time goes in v3:
time: 37 us; the launch traced here: 36.8 us
  Pallas kernels  35 us (95%)
  local copies, waits for them, and re-layouts  1.77 us (5%)
    pallas_call x1, Pallas kernels, per_device(): pl.pallas_call(functools.partial(kernel, n), out_shape=jax.ShapeDtypeStru...  35 us
    unnamed x1, local copies, waits for them, and re-layouts  1.77 us

profile of v3, /device:TPU:0, one launch (start us, length us, event | category | flops | bytes accessed | tf_op | source)
XLA Modules:
  0.0 36.8 jit_solution(6753091101105594021)
XLA Ops:
  0.0 35.0 %shard_map.100 = f32[64,1536]{1,0:T(8,128)} custom-call(bf16[2,64,1536]{2,1,0:T(8,128)(2,1)} %hidden_ref.1, s32[2,64]{1,0:T(2,128)} %ids_ref.1, bf16[1536]{0:T(1024)(128)(2,1)} %attn_gain_ref.1, bf16[1536,768]{1,0:T(8,128)(2,1)} %q_hbm.1, bf16[1536,384]{1,0:T(8,128)(2,1)} %kv_hbm.1, bf16[768,1536]{1,0:T(8,128)(2,1)} %out_hbm.1, ...), custom_call_target="tpu_custom_call" | custom-call | tf_op jit(solution)/shard_map/pallas_call | solution.py:424
  35.1 1.8 %copy.12 = f32[64,1536]{1,0:T(8,128)} copy(f32[64,1536]{1,0:T(8,128)} %shard_map.100) | data formatting | bytes 786432

commit v4 on v3

--- a/solution.py
+++ b/solution.py
@@ -28,7 +28,7 @@
 
 
 def softplus(v):
-    return jnp.maximum(v, 0.0) + jnp.log1p(jnp.exp(-jnp.abs(v)))
+    return jnp.maximum(v, 0.0) + jnp.log(1.0 + jnp.exp(-jnp.abs(v)))
 
 
 def vector(ref):
@@ -57,7 +57,6 @@
     perm_w,
     buf,
     stage,
-    scores,
     att,
     final,
     other,
@@ -98,7 +97,9 @@
     skip_right, skip_left = even & (z < line - 2), odd & (z > 1)
 
     def slot(zc, xc, cc):
-        return (zc * 2 + xc) * 2 + cc
+        return (xc * line + zc) * 2 + cc
+
+    mine_at, pair_at = slot(z, x, core), slot(z, x, 1 - core)
 
     def remote(src, dst, send_sem, recv_sem, device):
         return pltpu.make_async_remote_copy(
@@ -179,8 +180,8 @@
     def to_across(zc, half):
         return piece(slot(zc, x, half), across, send_x.at[half, zc])
 
-    pair = remote(stage, buf.at[me], pair_sem.at[0], recv.at[me], sibling)
-    pair_in = remote(stage, buf.at[sibling], pair_sem.at[0], recv.at[sibling], sibling)
+    pair = remote(stage, buf.at[mine_at], pair_sem.at[0], recv.at[mine_at], sibling)
+    pair_in = remote(stage, buf.at[pair_at], pair_sem.at[0], recv.at[pair_at], sibling)
 
     out_zero = jnp.zeros((pad, width), jnp.bfloat16)
     for h in range(heads):
@@ -196,7 +197,7 @@
     flag = jnp.where(ids_ref[...] != 4, 1.0, 0.0).astype(jnp.float32)
     per_tile = LANES // rows
     lane = lax.broadcasted_iota(jnp.int32, (1, LANES), 1)
-    start = lax.rem(me, per_tile) * rows
+    start = lax.rem(mine_at, per_tile) * rows
     inside_tile = (lane >= start) & (lane < start + rows)
 
     def fill(block, values, flags):
@@ -208,7 +209,7 @@
 
     fill(stage, theirs, jnp.where(first, flag[1:2], flag[0:1]))
     pair.start()
-    fill(buf.at[me], mine, jnp.where(first, flag[0:1], flag[1:2]))
+    fill(buf.at[mine_at], mine, jnp.where(first, flag[0:1], flag[1:2]))
 
     def spread_out(zc, half, go_left, go_right):
         source = go_left and go_right
@@ -267,84 +268,76 @@
             perm_w[pl.ds(pl.multiple_of(base, chunk), chunk), :] = hit.astype(jnp.bfloat16)
         return 0
 
+    def make_queries():
+        load_q.wait()
+        pltpu.make_async_copy(hidden_ref.at[0], lower, work_sem.at[0]).wait()
+        swap_upper.wait_recv()
+        return project_queries(normalize(work[...], gain))
+
     if line <= 4:
         for d in range(1, line):
             hop(d)
+            if d == 1:
+                build_perm(0, 0)
+                build_perm(1, 0)
+            if d == line - 2:
+                build_perm(2, 0)
+                build_perm(3, 0)
+                queries = make_queries()
     else:
         pl.loop(1, line)(hop)
-
-    @pl.when(second)
-    def _():
+    if not 3 <= line <= 4:
         lax.fori_loop(0, 4, build_perm, 0)
-
-    load_q.wait()
-    pltpu.make_async_copy(hidden_ref.at[0], lower, work_sem.at[0]).wait()
-    swap_upper.wait_recv()
-    queries = project_queries(normalize(work[...], gain))
+        queries = make_queries()
+
+    blocks = 2 * line
+    keys = blocks * rows
+    scale = 1.0 / math.sqrt(head_dim)
+
+    def part(column):
+        at = pl.ds(column * blocks, blocks)
+
+        def tiles(low, high):
+            parts = [
+                buf[at, pl.ds(j * rows, rows), :].reshape(keys, LANES) for j in range(low, high)
+            ]
+            return jnp.concatenate(parts, axis=1)
+
+        flags = buf[at, pl.ds(kv_tiles * rows, FLAG_ROWS), :].astype(jnp.float32)
+        parts = []
+        for g in range(blocks // per_tile):
+            row = flags[g * per_tile, 0:1, :]
+            for k in range(1, per_tile):
+                row = row + flags[g * per_tile + k, 0:1, :]
+            parts.append(row)
+        usable = jnp.concatenate(parts, axis=1) > 0.5
+        lhs = tiles(0, padded // LANES)
+        rhs = tiles(kv_tiles - padded // LANES, kv_tiles)
+        states = []
+        for h in range(heads):
+            value = jnp.where(usable, dot_t(queries[h], lhs) * scale, -1e30)
+            top = jnp.max(value, -1, keepdims=True)
+            weight = jnp.where(usable, jnp.exp(value - top), 0.0)
+            total = jnp.sum(weight, -1, keepdims=True)
+            states.append((top, total, dot(weight.astype(jnp.bfloat16), rhs)))
+        return states
+
+    near = part(x)
 
     @pl.loop(0, line)
     def _(zc):
         for half in range(2):
             piece(slot(zc, 1 - x, half), across, send_x.at[half, zc]).wait_recv()
 
-    chunk_blocks = min(n, 1024 // rows)
-    chunk_keys = chunk_blocks * rows
-    chunks = n // chunk_blocks
-    scale = 1.0 / math.sqrt(head_dim)
-
-    def tiles(c, low, high):
-        at = pl.ds(c * chunk_blocks, chunk_blocks)
-        return jnp.concatenate(
-            [
-                buf[at, pl.ds(j * rows, rows), :].reshape(chunk_keys, LANES)
-                for j in range(low, high)
-            ],
-            axis=1,
-        )
-
-    def usable(c):
-        at = pl.ds(c * chunk_blocks, chunk_blocks)
-        flags = buf[at, pl.ds(kv_tiles * rows, FLAG_ROWS), :].astype(jnp.float32)
-        parts = []
-        for g in range(chunk_blocks // per_tile):
-            row = flags[g * per_tile, 0:1, :]
-            for k in range(1, per_tile):
-                row = row + flags[g * per_tile + k, 0:1, :]
-            parts.append(row)
-        return jnp.concatenate(parts, axis=1) > 0.5
-
-    def score(c, q):
-        return jnp.where(usable(c), dot_t(q, tiles(c, 0, padded // LANES)) * scale, -1e30)
-
-    def weigh(c, value, top):
-        weight = jnp.where(usable(c), jnp.exp(value - top), 0.0)
-        rhs = tiles(c, kv_tiles - padded // LANES, kv_tiles)
-        return jnp.sum(weight, -1, keepdims=True), dot(weight.astype(jnp.bfloat16), rhs)
-
+    distant = part(1 - x)
     inside = lax.broadcasted_iota(jnp.int32, (both, padded), 1) >= pad
     for h in range(heads):
-        if chunks == 1:
-            value = score(0, queries[h])
-            total, summed = weigh(0, value, jnp.max(value, -1, keepdims=True))
-        else:
-
-            def first_pass(c, top):
-                value = score(c, queries[h])
-                scores[c] = value
-                return jnp.maximum(top, jnp.max(value, -1, keepdims=True))
-
-            top = lax.fori_loop(
-                0, chunks, first_pass, jnp.full((both, 1), -1e30, jnp.float32)
-            )
-
-            def second_pass(c, state):
-                total, summed = weigh(c, scores[c], top)
-                return state[0] + total, state[1] + summed
-
-            empty = jnp.zeros((both, 1), jnp.float32), jnp.zeros((both, padded), jnp.float32)
-            total, summed = lax.fori_loop(0, chunks, second_pass, empty)
-        mixed = jnp.where(inside, summed / total, 0.0)
-        att[:, pl.ds(h * padded, padded)] = mixed.astype(jnp.bfloat16)
+        (top_a, total_a, sum_a), (top_b, total_b, sum_b) = near[h], distant[h]
+        top = jnp.maximum(top_a, top_b)
+        scale_a, scale_b = jnp.exp(top_a - top), jnp.exp(top_b - top)
+        total = total_a * scale_a + total_b * scale_b
+        mixed = (sum_a * scale_a + sum_b * scale_b) / total
+        att[:, pl.ds(h * padded, padded)] = jnp.where(inside, mixed, 0.0).astype(jnp.bfloat16)
 
     for load in load_out:
         load.wait()
@@ -367,14 +360,25 @@
             0.0,
         ).astype(jnp.bfloat16)
         flipped = dot(flip, pred).astype(jnp.bfloat16)
-        final[...] = dot(flipped, perm_w[...]).astype(jnp.bfloat16)
+        final[...] = flipped
 
     own = pl.ds(pl.multiple_of(core * rows, rows), rows)
     far = pl.ds(pl.multiple_of(rows - core * rows, rows), rows)
     exchange = remote(final.at[far], other, final_sem.at[0], final_sem.at[1], sibling)
     exchange.start()
-    exchange.wait_recv()
-    result_ref[...] = 0.5 * (final[own, :].astype(jnp.float32) + other[...].astype(jnp.float32))
+
+    @pl.when(first)
+    def _():
+        exchange.wait_recv()
+        result_ref[...] = 0.5 * (
+            final[own, :].astype(jnp.float32) + dot(other[...], perm_w[...])
+        )
+
+    @pl.when(second)
+    def _():
+        turned = dot(final[own, :], perm_w[...])
+        exchange.wait_recv()
+        result_ref[...] = 0.5 * (other[...].astype(jnp.float32) + turned)
 
     exchange.wait_send()
     pair.wait_send()
@@ -415,12 +419,9 @@
     padded = -(-head_dim // LANES) * LANES
     line = n // 4
     kv_rows = kv_weight.shape[1] // LANES * rows
-    chunk_blocks = min(n, 1024 // rows)
-    chunks = n // chunk_blocks
     bf16 = jnp.bfloat16
     vmem = pl.BlockSpec(memory_space=pltpu.VMEM)
     hbm = pl.BlockSpec(memory_space=pl.ANY)
-    score_shape = (chunks, 2 * rows, chunk_blocks * rows) if chunks > 1 else (1, 8, LANES)
     return pl.pallas_call(
         functools.partial(kernel, n),
         out_shape=jax.ShapeDtypeStruct((rows, tracks), jnp.float32),
@@ -436,7 +437,6 @@
             pltpu.VMEM((tracks, tracks), bf16),
             pltpu.VMEM((n, kv_rows + FLAG_ROWS, LANES), bf16),
             pltpu.VMEM((kv_rows + FLAG_ROWS, LANES), bf16),
-            pltpu.VMEM(score_shape, jnp.float32),
             pltpu.VMEM((2 * rows, heads * padded), bf16),
             pltpu.VMEM((2 * rows, tracks), bf16),
             pltpu.VMEM((rows, tracks), bf16),

time: 37 us -> 36.7 us (level)
  no operation moved by 1% of the time
where the time goes in v4:
time: 36.7 us; the launch traced here: 36.5 us
  Pallas kernels  34.7 us (95%)
  local copies, waits for them, and re-layouts  1.77 us (5%)
    pallas_call x1, Pallas kernels, per_device(): pl.pallas_call(functools.partial(kernel, n), out_shape=jax.ShapeDtypeStru...  34.7 us
    unnamed x1, local copies, waits for them, and re-layouts  1.77 us

profile of v4, /device:TPU:0, one launch (start us, length us, event | category | flops | bytes accessed | tf_op | source)
XLA Modules:
  0.0 36.5 jit_solution(10935850240660912873)
XLA Ops:
  0.0 34.7 %shard_map.100 = f32[64,1536]{1,0:T(8,128)} custom-call(bf16[2,64,1536]{2,1,0:T(8,128)(2,1)} %hidden_ref.1, s32[2,64]{1,0:T(2,128)} %ids_ref.1, bf16[1536]{0:T(1024)(128)(2,1)} %attn_gain_ref.1, bf16[1536,768]{1,0:T(8,128)(2,1)} %q_hbm.1, bf16[1536,384]{1,0:T(8,128)(2,1)} %kv_hbm.1, bf16[768,1536]{1,0:T(8,128)(2,1)} %out_hbm.1, ...), custom_call_target="tpu_custom_call" | custom-call | tf_op jit(solution)/shard_map/pallas_call | solution.py:425
  34.7 1.8 %copy.12 = f32[64,1536]{1,0:T(8,128)} copy(f32[64,1536]{1,0:T(8,128)} %shard_map.100) | data formatting | bytes 786432

commit v5 on v4

--- a/solution.py
+++ b/solution.py
@@ -69,8 +69,6 @@
     recv,
     send_l,
     send_r,
-    send_ll,
-    send_rr,
     send_x,
 ):
     line = n // 4
@@ -92,9 +90,6 @@
     first = core == 0
     second = core == 1
     has_left, has_right = z > 0, z < line - 1
-    even = lax.rem(z, 2) == 0
-    odd = lax.rem(z, 2) == 1
-    skip_right, skip_left = even & (z < line - 2), odd & (z > 1)
 
     def slot(zc, xc, cc):
         return (xc * line + zc) * 2 + cc
@@ -135,15 +130,13 @@
     greet(across)
     pl.when(has_left)(lambda: greet(left))
     pl.when(has_right)(lambda: greet(right))
-    pl.when(even & (z > 1))(lambda: greet(me - 8))
-    pl.when(odd & (z < line - 2))(lambda: greet(me + 8))
 
     @pl.when(second)
     def _():
         greet(mirror_zero)
         greet(mirror_one)
 
-    peers = [flag.astype(jnp.int32) for flag in (has_left, has_right, skip_left, skip_right)]
+    peers = [flag.astype(jnp.int32) for flag in (has_left, has_right)]
     pl.semaphore_wait(barrier, 3 + sum(peers))
 
     lower, upper = work.at[pl.ds(0, rows)], work.at[pl.ds(rows, rows)]
@@ -170,12 +163,6 @@
 
     def to_right(zc, half):
         return piece(slot(zc, x, half), right, send_r.at[half, zc])
-
-    def to_left_two(zc, half):
-        return piece(slot(zc, x, half), me - 8, send_ll.at[half, zc])
-
-    def to_right_two(zc, half):
-        return piece(slot(zc, x, half), me + 8, send_rr.at[half, zc])
 
     def to_across(zc, half):
         return piece(slot(zc, x, half), across, send_x.at[half, zc])
@@ -212,17 +199,10 @@
     fill(buf.at[mine_at], mine, jnp.where(first, flag[0:1], flag[1:2]))
 
     def spread_out(zc, half, go_left, go_right):
-        source = go_left and go_right
         if go_left:
-            pl.when(skip_left)(lambda: to_left_two(zc, half).start())
-            pl.when(has_left if source else has_left & odd)(
-                lambda: to_left(zc, half).start()
-            )
+            pl.when(has_left)(lambda: to_left(zc, half).start())
         if go_right:
-            pl.when(skip_right)(lambda: to_right_two(zc, half).start())
-            pl.when(has_right if source else has_right & even)(
-                lambda: to_right(zc, half).start()
-            )
+            pl.when(has_right)(lambda: to_right(zc, half).start())
         to_across(zc, half).start()
 
     spread_out(z, core, True, True)
@@ -283,12 +263,11 @@
             if d == line - 2:
                 build_perm(2, 0)
                 build_perm(3, 0)
-                queries = make_queries()
     else:
         pl.loop(1, line)(hop)
     if not 3 <= line <= 4:
         lax.fori_loop(0, 4, build_perm, 0)
-        queries = make_queries()
+    queries = make_queries()
 
     blocks = 2 * line
     keys = blocks * rows
@@ -388,14 +367,8 @@
     @pl.loop(0, line)
     def _(zc):
         for half in range(2):
-            pl.when(has_right & ((zc == z) | (even & (zc < z))))(
-                lambda: to_right(zc, half).wait_send()
-            )
-            pl.when(has_left & ((zc == z) | (odd & (zc > z))))(
-                lambda: to_left(zc, half).wait_send()
-            )
-            pl.when(skip_right & (zc <= z))(lambda: to_right_two(zc, half).wait_send())
-            pl.when(skip_left & (zc >= z))(lambda: to_left_two(zc, half).wait_send())
+            pl.when(has_right & (zc <= z))(lambda: to_right(zc, half).wait_send())
+            pl.when(has_left & (zc >= z))(lambda: to_left(zc, half).wait_send())
             to_across(zc, half).wait_send()
 
 
@@ -450,8 +423,6 @@
             pltpu.SemaphoreType.DMA((2, line)),
             pltpu.SemaphoreType.DMA((2, line)),
             pltpu.SemaphoreType.DMA((2, line)),
-            pltpu.SemaphoreType.DMA((2, line)),
-            pltpu.SemaphoreType.DMA((2, line)),
         ],
         compiler_params=pltpu.CompilerParams(
             collective_id=0, has_side_effects=True, vmem_limit_bytes=60 * 1024 * 1024

time: 36.7 us -> 34.5 us (0.940)
  Pallas kernels: 34.7 us -> 32.5 us
    pallas_call x1, Pallas kernels: 34.7 us -> 32.5 us  [per_device(): pl.pallas_call(functools.partial(kernel, n), out_shape=jax.ShapeDtypeStru...]
where the time goes in v5:
time: 34.5 us; the launch traced here: 34.3 us
  Pallas kernels  32.5 us (94%)
  local copies, waits for them, and re-layouts  1.77 us (5%)
    pallas_call x1, Pallas kernels, per_device(): pl.pallas_call(functools.partial(kernel, n), out_shape=jax.ShapeDtypeStru...  32.5 us
    unnamed x1, local copies, waits for them, and re-layouts  1.77 us

profile of v5, /device:TPU:0, one launch (start us, length us, event | category | flops | bytes accessed | tf_op | source)
XLA Modules:
  0.0 34.3 jit_solution(4492291362860592566)
XLA Ops:
  0.0 32.5 %shard_map.100 = f32[64,1536]{1,0:T(8,128)} custom-call(bf16[2,64,1536]{2,1,0:T(8,128)(2,1)} %hidden_ref.1, s32[2,64]{1,0:T(2,128)} %ids_ref.1, bf16[1536]{0:T(1024)(128)(2,1)} %attn_gain_ref.1, bf16[1536,768]{1,0:T(8,128)(2,1)} %q_hbm.1, bf16[1536,384]{1,0:T(8,128)(2,1)} %kv_hbm.1, bf16[768,1536]{1,0:T(8,128)(2,1)} %out_hbm.1, ...), custom_call_target="tpu_custom_call" | custom-call | tf_op jit(solution)/shard_map/pallas_call | solution.py:398
  32.5 1.8 %copy.12 = f32[64,1536]{1,0:T(8,128)} copy(f32[64,1536]{1,0:T(8,128)} %shard_map.100) | data formatting | bytes 786432

commit v6 on v5

--- a/solution.py
+++ b/solution.py
@@ -139,21 +139,37 @@
     peers = [flag.astype(jnp.int32) for flag in (has_left, has_right)]
     pl.semaphore_wait(barrier, 3 + sum(peers))
 
-    lower, upper = work.at[pl.ds(0, rows)], work.at[pl.ds(rows, rows)]
-    keep_own = pltpu.make_async_copy(hidden_ref.at[0], lower, work_sem.at[0])
-    give_pair = remote(hidden_ref.at[0], upper, swap_send.at[0], work_sem.at[1], sibling)
-    swap_lower = remote(hidden_ref.at[1], lower, swap_send.at[1], work_sem.at[0], mirror_one)
-    swap_upper = remote(hidden_ref.at[1], upper, swap_send.at[1], work_sem.at[1], mirror_one)
+    cuts = work_sem.shape[1]
+    cut = rows // cuts
+
+    def share(strand, side, j, device):
+        return remote(
+            hidden_ref.at[strand, pl.ds(j * cut, cut)],
+            work.at[pl.ds(side * rows + j * cut, cut)],
+            swap_send.at[strand, j],
+            work_sem.at[side, j],
+            device,
+        )
+
+    def keep(j):
+        return pltpu.make_async_copy(
+            hidden_ref.at[0, pl.ds(j * cut, cut)],
+            work.at[pl.ds(j * cut, cut)],
+            work_sem.at[0, j],
+        )
+
+    def send_swap(j):
+        pl.when(first)(lambda: share(1, 0, j, mirror_one).start())
+        pl.when(second)(lambda: share(1, 1, j, mirror_one).start())
 
     @pl.when(first)
     def _():
-        keep_own.start()
-        swap_lower.start()
-
-    @pl.when(second)
-    def _():
-        give_pair.start()
-        swap_upper.start()
+        for j in range(cuts):
+            keep(j).start()
+
+    early = (cuts + 1) // 2
+    for j in range(early):
+        send_swap(j)
 
     def piece(index, device, send_sem):
         return remote(buf.at[index], buf.at[index], send_sem, recv.at[index], device)
@@ -209,6 +225,15 @@
     pair_in.wait_recv()
     spread_out(z, 1 - core, True, True)
 
+    @pl.when(second)
+    def _():
+        for j in range(cuts):
+            share(0, 1, j, sibling).start()
+
+    late = cuts if line > 4 or line < 3 else min(early + 1, cuts)
+    for j in range(early, late):
+        send_swap(j)
+
     def hop(d):
         for k in range(2):
             half = core if k == 0 else 1 - core
@@ -250,14 +275,17 @@
 
     def make_queries():
         load_q.wait()
-        pltpu.make_async_copy(hidden_ref.at[0], lower, work_sem.at[0]).wait()
-        swap_upper.wait_recv()
+        for j in range(cuts):
+            keep(j).wait()
+            share(1, 1, j, mirror_one).wait_recv()
         return project_queries(normalize(work[...], gain))
 
     if line <= 4:
         for d in range(1, line):
             hop(d)
             if d == 1:
+                for j in range(late, cuts):
+                    send_swap(j)
                 build_perm(0, 0)
                 build_perm(1, 0)
             if d == line - 2:
@@ -361,8 +389,9 @@
 
     exchange.wait_send()
     pair.wait_send()
-    swap_upper.wait_send()
-    pl.when(second)(lambda: give_pair.wait_send())
+    for j in range(cuts):
+        share(1, 1, j, mirror_one).wait_send()
+        pl.when(second)(lambda: share(0, 1, j, sibling).wait_send())
 
     @pl.loop(0, line)
     def _(zc):
@@ -392,6 +421,7 @@
     padded = -(-head_dim // LANES) * LANES
     line = n // 4
     kv_rows = kv_weight.shape[1] // LANES * rows
+    cuts = 4 if rows % 64 == 0 else 1
     bf16 = jnp.bfloat16
     vmem = pl.BlockSpec(memory_space=pltpu.VMEM)
     hbm = pl.BlockSpec(memory_space=pl.ANY)
@@ -415,8 +445,8 @@
             pltpu.VMEM((rows, tracks), bf16),
             pltpu.SemaphoreType.DMA((4,)),
             pltpu.SemaphoreType.DMA((heads,)),
-            pltpu.SemaphoreType.DMA((2,)),
-            pltpu.SemaphoreType.DMA((2,)),
+            pltpu.SemaphoreType.DMA((2, cuts)),
+            pltpu.SemaphoreType.DMA((2, cuts)),
             pltpu.SemaphoreType.DMA((1,)),
             pltpu.SemaphoreType.DMA((2,)),
             pltpu.SemaphoreType.DMA((n,)),

time: 34.5 us -> 33.3 us (0.965)
  Pallas kernels: 32.5 us -> 31.3 us
    pallas_call x1, Pallas kernels: 32.5 us -> 31.3 us  [per_device(): pl.pallas_call(functools.partial(kernel, n), out_shape=jax.ShapeDtypeStru...]
where the time goes in v6:
time: 33.3 us; the launch traced here: 33.1 us
  Pallas kernels  31.3 us (94%)
  local copies, waits for them, and re-layouts  1.77 us (5%)
    pallas_call x1, Pallas kernels, per_device(): pl.pallas_call(functools.partial(kernel, n), out_shape=jax.ShapeDtypeStru...  31.3 us
    unnamed x1, local copies, waits for them, and re-layouts  1.77 us

profile of v6, /device:TPU:0, one launch (start us, length us, event | category | flops | bytes accessed | tf_op | source)
XLA Modules:
  0.0 33.1 jit_solution(10485727586716490946)
XLA Ops:
  0.0 31.3 %shard_map.100 = f32[64,1536]{1,0:T(8,128)} custom-call(bf16[2,64,1536]{2,1,0:T(8,128)(2,1)} %hidden_ref.1, s32[2,64]{1,0:T(2,128)} %ids_ref.1, bf16[1536]{0:T(1024)(128)(2,1)} %attn_gain_ref.1, bf16[1536,768]{1,0:T(8,128)(2,1)} %q_hbm.1, bf16[1536,384]{1,0:T(8,128)(2,1)} %kv_hbm.1, bf16[768,1536]{1,0:T(8,128)(2,1)} %out_hbm.1, ...), custom_call_target="tpu_custom_call" | custom-call | tf_op jit(solution)/shard_map/pallas_call | solution.py:428
  31.3 1.8 %copy.12 = f32[64,1536]{1,0:T(8,128)} copy(f32[64,1536]{1,0:T(8,128)} %shard_map.100) | data formatting | bytes 786432

commit v7 on v6

--- a/solution.py
+++ b/solution.py
@@ -167,7 +167,7 @@
         for j in range(cuts):
             keep(j).start()
 
-    early = (cuts + 1) // 2
+    early = 1
     for j in range(early):
         send_swap(j)
 
@@ -230,7 +230,7 @@
         for j in range(cuts):
             share(0, 1, j, sibling).start()
 
-    late = cuts if line > 4 or line < 3 else min(early + 1, cuts)
+    late = cuts if line > 4 or line < 3 else min(early + 2, cuts)
     for j in range(early, late):
         send_swap(j)
 

time: 33.3 us -> 33.3 us (level)
  no operation moved by 1% of the time
where the time goes in v7:
time: 33.3 us; the launch traced here: 33.1 us
  Pallas kernels  31.3 us (94%)
  local copies, waits for them, and re-layouts  1.77 us (5%)
    pallas_call x1, Pallas kernels, per_device(): pl.pallas_call(functools.partial(kernel, n), out_shape=jax.ShapeDtypeStru...  31.3 us
    unnamed x1, local copies, waits for them, and re-layouts  1.77 us

profile of v7, /device:TPU:0, one launch (start us, length us, event | category | flops | bytes accessed | tf_op | source)
XLA Modules:
  0.0 33.1 jit_solution(13674281264240065166)
XLA Ops:
  0.0 31.3 %shard_map.100 = f32[64,1536]{1,0:T(8,128)} custom-call(bf16[2,64,1536]{2,1,0:T(8,128)(2,1)} %hidden_ref.1, s32[2,64]{1,0:T(2,128)} %ids_ref.1, bf16[1536]{0:T(1024)(128)(2,1)} %attn_gain_ref.1, bf16[1536,768]{1,0:T(8,128)(2,1)} %q_hbm.1, bf16[1536,384]{1,0:T(8,128)(2,1)} %kv_hbm.1, bf16[768,1536]{1,0:T(8,128)(2,1)} %out_hbm.1, ...), custom_call_target="tpu_custom_call" | custom-call | tf_op jit(solution)/shard_map/pallas_call | solution.py:428
  31.3 1.8 %copy.12 = f32[64,1536]{1,0:T(8,128)} copy(f32[64,1536]{1,0:T(8,128)} %shard_map.100) | data formatting | bytes 786432
